TPU v7x, 32 devices: a whole 2x2x4 slice. The times are simulated.
32 devices in a mesh: seq: 4 (over z), head: 4 (over y, core), req: 2 (over x).
Axes of the slice: x: 2, y: 2, z: 4, core: 2. Of those that a mesh axis runs over, the one named last changes fastest.
Arguments:
- pre_qkv: bfloat16 [8192, 3, 4096], P('seq', None, ('head', 'req')), may hold values from -200 to 200
- cache_kv: bfloat16 [8, 2, 256, 4096], P('req', None, 'seq', 'head'), may hold values from -6 to 6
- dec_new: bfloat16 [16, 3, 2, 4096], P('req', None, None, 'head'), may hold values from -200 to 200
- out_weight: bfloat16 [4096, 4096], P('head', 'seq'), may hold values from -0.09375 to 0.09375
- owner_slot: int32 [8], replicated, may hold values from 0 to 15, as said below
- prompt_lengths: int32 [8], replicated, may hold values from 1 to 256
Outputs:
- prefill_out: bfloat16 [8192, 4096], P('seq', ('head', 'req'))
- decode_out: bfloat16 [16, 2, 4096], P('req', None, ('seq', 'head'))
Inputs may be any that keep to these rules, and one draw needn't show every extreme that they name: `owner_slot`: distinct slots; slot s belongs to decode group s // 8. Of the requests of one aligned block of 4, at most 4 are owned by one group, and the last group, 1, owns exactly 4 from every block.
All inputs are finite; a program needn't handle non-finite values.
Results may differ from a plain program's by a relative error of at most 0.012.
Values may be sent and summed in bfloat16 or wider, within the bound.
A program may use at most 128 MiB of HBM per device.

v0:
```python
import functools
from functools import reduce

import jax
import jax.numpy as jnp
from jax import lax
from jax.experimental import pallas as pl
from jax.experimental.pallas import tpu as pltpu
from jax.sharding import PartitionSpec as P

HEAD_DIM = 128
LOG2E = 1.4426950408889634


NEG_FILL = -1e30


def merged_2(value, axis, join):
    pieces = jax.tree.map(lambda part: lax.all_gather(part, axis), value)
    head = jax.tree.map(lambda part: part[0], pieces)
    tail = jax.tree.map(lambda part: part[1:], pieces)
    total, _ = lax.scan(lambda total, section: (join(total, section), None), head, tail)
    return total


def partial_block(query_rows, key_rows, value_rows, allowed):
    score_scale = query_rows.shape[-1] ** (-0.5)
    scores = (
        jnp.einsum("qhd,khd->hqk", query_rows, key_rows, preferred_element_type=jnp.float32)
        * score_scale
    )
    scores = jnp.where(allowed, scores, NEG_FILL)
    peak_score = jnp.max(scores, axis=-1)
    weights = jnp.where(allowed, jnp.exp(scores - peak_score[..., None]), 0.0)
    weight_sum = jnp.sum(weights, axis=-1)
    value_sum = jnp.einsum(
        "hqk,khd->hqd", weights.astype(jnp.bfloat16), value_rows, preferred_element_type=jnp.float32
    )
    return (peak_score, weight_sum, value_sum)


def pick_rows(field, stride, residue):
    row_count, head_count, width = field.shape
    shaped = field.reshape(row_count // stride, stride, head_count, width)
    member = (jnp.arange(stride)[:, None] == residue[None, :])[None, :, :, None]
    return jnp.sum(jnp.where(member, shaped, jnp.zeros((), field.dtype)), axis=1)


def spread_rows(level_term, stride, residue):
    peak_score, weight_sum, value_sum = level_term
    head_count, sparse_count = peak_score.shape
    member = jnp.arange(stride)[:, None] == residue[None, :]
    peak_rows = jnp.where(member[None], peak_score.T[:, None, :], NEG_FILL).reshape(
        sparse_count * stride, head_count
    )
    sum_rows = jnp.where(member[None], weight_sum.T[:, None, :], 0.0).reshape(
        sparse_count * stride, head_count
    )
    value_rows = jnp.where(member[None, :, :, None], jnp.swapaxes(value_sum, 0, 1)[:, None], 0.0)
    return (peak_rows, sum_rows, value_rows.reshape(sparse_count * stride, head_count, -1))


def combine_levels(levels):
    top_all = reduce(jnp.maximum, [level_term[0] for level_term in levels])
    numerator = 0.0
    denominator = 0.0
    for peak_score, weight_sum, value_sum in levels:
        factor = jnp.exp(peak_score - top_all)
        denominator = denominator + weight_sum * factor
        numerator = numerator + value_sum * factor[..., None]
    return numerator / denominator[..., None]


def merge_pair(earlier_part, later_part):
    top_both = jnp.maximum(earlier_part[0], later_part[0])
    factor_one = jnp.exp(earlier_part[0] - top_both)
    factor_two = jnp.exp(later_part[0] - top_both)
    weight_sum = earlier_part[1] * factor_one + later_part[1] * factor_two
    value_sum = earlier_part[2] * factor_one[..., None] + later_part[2] * factor_two[..., None]
    return (top_both, weight_sum, value_sum)


def causal_mask(query_count, key_count, offset):
    return jnp.arange(key_count)[None, :] <= (offset + jnp.arange(query_count))[:, None]


def prefill_block(pre_qkv):
    seq_index = lax.axis_index("seq")
    seq_count = lax.axis_size("seq")
    head_index = lax.axis_index(("head", "req"))
    row_count = pre_qkv.shape[0]
    width = pre_qkv.shape[2]
    head_count = width // HEAD_DIM
    head_ids = head_index * head_count + jnp.arange(head_count)
    query_rows = pre_qkv[:, 0].reshape(row_count, head_count, HEAD_DIM)
    key_rows = pre_qkv[:, 1].reshape(row_count, head_count, HEAD_DIM)
    value_rows = pre_qkv[:, 2].reshape(row_count, head_count, HEAD_DIM)
    zero_residue = jnp.zeros((head_count,), jnp.int32)
    residue_four = head_ids % 4
    residue_far = head_ids % seq_count
    block_rows = min(512, row_count)
    block_count = row_count // block_rows

    def near_part(packed):
        query_block, start_row = packed
        return partial_block(
            query_block, key_rows, value_rows, causal_mask(block_rows, row_count, start_row)
        )

    block_starts = jnp.arange(block_count, dtype=jnp.int32) * block_rows
    near_peak, near_sum, near_value = lax.map(
        near_part, (query_rows.reshape(block_count, block_rows, head_count, HEAD_DIM), block_starts)
    )
    near_term = (
        jnp.moveaxis(near_peak, 0, 1).reshape(head_count, row_count),
        jnp.moveaxis(near_sum, 0, 1).reshape(head_count, row_count),
        jnp.moveaxis(near_value, 0, 1).reshape(head_count, row_count, HEAD_DIM),
    )
    levels = [spread_rows(near_term, 1, zero_residue)]
    keys_four = pick_rows(key_rows, 4, residue_four)
    values_four = pick_rows(value_rows, 4, residue_four)
    every_keys, every_values = (
        lax.all_gather(keys_four, "seq", axis=0, tiled=True),
        lax.all_gather(values_four, "seq", axis=0, tiled=True),
    )
    start_row = seq_index // 4 * row_count
    group_keys = lax.dynamic_slice_in_dim(every_keys, start_row, row_count, 0)
    group_values = lax.dynamic_slice_in_dim(every_values, start_row, row_count, 0)
    inner_residue = residue_far // 4
    far_keys = pick_rows(every_keys, seq_count // 4, inner_residue)
    far_values = pick_rows(every_values, seq_count // 4, inner_residue)
    quarter = row_count // 4
    query_four = pick_rows(query_rows, 4, residue_four)
    mid_term = partial_block(
        query_four,
        group_keys,
        group_values,
        causal_mask(quarter, row_count, seq_index % 4 * quarter),
    )
    levels.append(spread_rows(mid_term, 4, residue_four))
    far_count = row_count // seq_count
    query_far = pick_rows(query_rows, seq_count, residue_far)
    far_term = partial_block(
        query_far, far_keys, far_values, causal_mask(far_count, row_count, seq_index * far_count)
    )
    levels.append(spread_rows(far_term, seq_count, residue_far))
    attended = combine_levels(levels)
    return attended.reshape(row_count, width).astype(jnp.bfloat16)


MESH = pl.DeviceIdType.MESH
F32 = jnp.float32
BF16 = jnp.bfloat16


def remote(source, target, send_sem, recv_sem, device):
    return pltpu.make_async_remote_copy(
        src_ref=source,
        dst_ref=target,
        send_sem=send_sem,
        recv_sem=recv_sem,
        device_id=device,
        device_id_type=MESH,
    )


def nt_dot(a, b):
    return lax.dot_general(a, b, (((1,), (1,)), ((), ())), preferred_element_type=F32)


def attend(query, parts):
    factor = HEAD_DIM ** (-0.5) * LOG2E
    scores = []
    for key, _, allowed in parts:
        block = nt_dot(query, key)
        scores.append(block if allowed is None else jnp.where(allowed, block, NEG_FILL))
    peak = reduce(jnp.maximum, [jnp.max(block, axis=1, keepdims=True) for block in scores])
    shift = peak * factor
    total = 0.0
    for block, (_, value, _) in zip(scores, parts):
        weights = jnp.exp2(block * factor - shift).astype(BF16)
        wide = jnp.concatenate([value, jnp.ones_like(value)], axis=1)
        total = total + jnp.dot(weights, wide, preferred_element_type=F32)
    weight_sum = total[:, HEAD_DIM:]
    return total[:, :HEAD_DIM] / weight_sum, shift + jnp.log2(weight_sum)


def triangle(rows):
    return lax.broadcasted_iota(jnp.int32, (rows, rows), 1) <= lax.broadcasted_iota(
        jnp.int32, (rows, rows), 0
    )


def prefill_kernel(
    qkv, out, near_o, near_l, wide, pick, kv_in, q_in, o_out, l_out, o_in, l_in,
    s_kv, r_kv, s_q, r_q, s_o, r_o, s_l, r_l,
):
    me = lax.axis_index("seq")
    row_count = qkv.shape[1]
    head_count = qkv.shape[2] // HEAD_DIM
    half = head_count // 2
    sparse = row_count // 4
    block = 256
    low, upper = pl.ds(0, half), pl.ds(half, half)

    barrier = pltpu.get_barrier_semaphore()
    for step in range(1, 4):
        pl.semaphore_signal(
            barrier, inc=1, device_id={"seq": lax.rem(me + step, 4)}, device_id_type=MESH
        )

    order = list(range(half, head_count)) + list(range(half))
    for head in order:
        lanes = pl.ds(head * HEAD_DIM, HEAD_DIM)
        for part in range(3):
            wide[...] = qkv[part, :, lanes].astype(F32)
            pick[part, head] = wide[pl.ds(head % 4, sparse, stride=4), :].astype(BF16)
    pl.semaphore_wait(barrier, 3)

    def kv_copy(heads, target):
        return remote(pick.at[pl.ds(1, 2), heads], kv_in, s_kv, r_kv, {"seq": target})

    def q_copy(heads, source, target):
        return remote(
            pick.at[0, heads], q_in.at[source - 1], s_q.at[target], r_q.at[source - 1],
            {"seq": target},
        )

    def o_copies(source, target):
        return (
            remote(
                o_out.at[target - 1], o_in.at[source], s_o.at[target - 1], r_o.at[source],
                {"seq": target},
            ),
            remote(
                l_out.at[target - 1], l_in.at[source], s_l.at[target - 1], r_l.at[source],
                {"seq": target},
            ),
        )

    sends = {
        0: [kv_copy(low, 1)],
        1: [q_copy(upper, 1, 0), kv_copy(upper, 0)],
        2: [q_copy(upper, 2, 0), q_copy(low, 2, 1), kv_copy(low, 3)],
        3: [q_copy(upper, 3, 0), q_copy(low, 3, 1), q_copy(upper, 3, 2)],
    }
    for index, copies in sends.items():

        @pl.when(me == index)
        def _(copies=copies):
            for copy in copies:
                copy.start()

    corner = triangle(block)

    def near(head):
        lanes = pl.ds(pl.multiple_of(head * HEAD_DIM, HEAD_DIM), HEAD_DIM)
        for at in range(row_count // block):
            here = pl.ds(at * block, block)
            parts = [(qkv[1, here, lanes], qkv[2, here, lanes], corner)]
            if at:
                before = pl.ds(0, at * block)
                parts.append((qkv[1, before, lanes], qkv[2, before, lanes], None))
            value, log_sum = attend(qkv[0, here, lanes], parts)
            near_o[head, here] = value
            near_l[head, here] = log_sum

    def near_heads(first, count):
        @pl.loop(first, first + count)
        def _(head):
            near(head)

    def merge(head, start, value, log_sum):
        rows = pl.ds(head % 4 + 4 * start, value.shape[0], stride=4)
        old_value, old_sum = near_o.at[head][rows, :], near_l.at[head][rows, :]
        both = log_sum + 1.0
        top = jnp.maximum(old_sum, both)
        one, two = jnp.exp2(old_sum - top), jnp.exp2(both - top)
        total = one + two
        near_o.at[head][rows, :] = (one * old_value + two * value) / total
        near_l.at[head][rows, :] = top + jnp.log2(total)

    def own_diagonal(head):
        for at in range(sparse // block):
            here = pl.ds(at * block, block)
            parts = [(pick[1, head, here], pick[2, head, here], corner)]
            if at:
                before = pl.ds(0, at * block)
                parts.append((pick[1, head, before], pick[2, head, before], None))
            merge(head, at * block, *attend(pick[0, head, here], parts))

    def serve(source, keys):
        for local in range(half):
            for at in range(sparse // block):
                here = pl.ds(at * block, block)
                value, log_sum = attend(q_in[source - 1, local, here], keys(local))
                o_out[source - 1, local, here] = value.astype(BF16)
                l_out[source - 1, local, :, here] = jnp.transpose(log_sum)[:8]

    def kept(first):
        return lambda local: [(pick[1, first + local], pick[2, first + local], None)]

    def landed(local):
        return [(kv_in[0, local], kv_in[1, local], None)]

    def extra():
        for local in range(half):
            for at in range(sparse // block):
                here = pl.ds(at * block, block)
                merge(local, at * block, *attend(pick[0, local, here], landed(local)))

    def send_back(source, target):
        for copy in o_copies(source, target):
            copy.start()

    near_heads(0, head_count)

    @pl.when(me == 0)
    def _():
        q_copy(upper, 1, 0).wait_recv()
        serve(1, kept(half))
        send_back(0, 1)
        kv_copy(upper, 0).wait_recv()
        for source in (2, 3):
            q_copy(upper, source, 0).wait_recv()
            serve(source, lambda local: kept(half)(local) + landed(local))
            send_back(0, source)

    @pl.when(me == 1)
    def _():
        kv_copy(low, 1).wait_recv()
        for source in (2, 3):
            q_copy(low, source, 1).wait_recv()
            serve(source, lambda local: kept(0)(local) + landed(local))
            send_back(1, source)
        extra()

    @pl.when(me == 2)
    def _():
        q_copy(upper, 3, 2).wait_recv()
        serve(3, kept(half))
        send_back(2, 3)

    @pl.when(me == 3)
    def _():
        kv_copy(low, 3).wait_recv()
        extra()

    for head in range(head_count):
        own_diagonal(head)

    arriving = {1: [(0, half)], 2: [(1, 0), (0, half)], 3: [(1, 0), (2, half), (0, half)]}
    for index, terms in arriving.items():

        @pl.when(me == index)
        def _(index=index, terms=terms):
            for source, first in terms:
                for copy in o_copies(source, index):
                    copy.wait_recv()
                for local in range(half):
                    rows = l_in[source, local]
                    log_sum = jnp.transpose(
                        jnp.concatenate([rows] * (HEAD_DIM // 8), axis=0)
                    )
                    merge(first + local, 0, o_in[source, local].astype(F32), log_sum)

    for head in range(head_count):
        out[:, pl.ds(head * HEAD_DIM, HEAD_DIM)] = near_o[head].astype(BF16)

    backs = {0: (1, 2, 3), 1: (2, 3), 2: (3,), 3: ()}
    for index, copies in sends.items():

        @pl.when(me == index)
        def _(index=index, copies=copies):
            for copy in copies:
                copy.wait_send()
            for target in backs[index]:
                for copy in o_copies(index, target):
                    copy.wait_send()


def prefill_fast(pre_qkv):
    qkv = jnp.moveaxis(pre_qkv, 1, 0)
    _, row_count, width = qkv.shape
    head_count = width // HEAD_DIM
    half, sparse = head_count // 2, row_count // 4
    dma = pltpu.SemaphoreType.DMA
    vmem = pltpu.VMEM
    return pl.pallas_call(
        prefill_kernel,
        out_shape=jax.ShapeDtypeStruct((row_count, width), BF16),
        in_specs=[pl.BlockSpec(memory_space=pltpu.VMEM)],
        out_specs=pl.BlockSpec(memory_space=pltpu.VMEM),
        scratch_shapes=[
            vmem((head_count, row_count, HEAD_DIM), F32),
            vmem((head_count, row_count, HEAD_DIM), F32),
            vmem((row_count, HEAD_DIM), F32),
            vmem((3, head_count, sparse, HEAD_DIM), BF16),
            vmem((2, half, sparse, HEAD_DIM), BF16),
            vmem((3, half, sparse, HEAD_DIM), BF16),
            vmem((3, half, sparse, HEAD_DIM), BF16),
            vmem((3, half, 8, sparse), F32),
            vmem((3, half, sparse, HEAD_DIM), BF16),
            vmem((3, half, 8, sparse), F32),
            dma, dma, dma((3,)), dma((3,)), dma((3,)), dma((3,)), dma((3,)), dma((3,)),
        ],
        compiler_params=pltpu.CompilerParams(
            collective_id=0, has_side_effects=True, vmem_limit_bytes=50 * 2**20
        ),
    )(qkv)


def decode_kernel(
    groups, seqs, heads,
    fresh, cache, weight, select, place, lengths, out,
    fresh_all, part_all, proj, proj_in, res_all,
    s_f, r_f, s_p, r_p, s_h, r_h, s_r, r_r,
):
    seq, head, req = lax.axis_index("seq"), lax.axis_index("head"), lax.axis_index("req")
    req_dev, _, rows_here, width = cache.shape
    head_count = width // HEAD_DIM
    items = 2 * req_dev
    columns = proj.shape[2]

    barrier = pltpu.get_barrier_semaphore()
    peers = [{"seq": lax.rem(seq + d, seqs)} for d in range(1, seqs)]
    peers += [{"head": lax.rem(head + d, heads)} for d in range(1, heads)]
    peers += [{"req": lax.rem(req + d, groups)} for d in range(1, groups)]
    for peer in peers:
        pl.semaphore_signal(barrier, inc=1, device_id=peer, device_id_type=MESH)
    pl.semaphore_wait(barrier, len(peers))

    fresh_copies = [
        remote(fresh, fresh_all.at[req], s_f.at[d - 1], r_f.at[d - 1],
               {"req": lax.rem(req + d, groups)})
        for d in range(1, groups)
    ]
    for copy in fresh_copies:
        copy.start()
    fresh_all[req] = fresh[...]
    for copy in fresh_copies:
        copy.wait_recv()

    def chosen(part):
        total = 0.0
        for group in range(groups):
            total = total + jnp.dot(select[group], fresh_all[group, part], preferred_element_type=F32)
        return total

    queries = chosen(0)
    new_keys, new_values = chosen(1).astype(BF16), chosen(2).astype(BF16)
    big = 2 * head_count
    row = lax.broadcasted_iota(jnp.int32, (big, width), 0)
    lane = lax.broadcasted_iota(jnp.int32, (big, width), 1)
    own_head = lax.rem(row, head_count) == lane // HEAD_DIM
    factor = HEAD_DIM ** (-0.5) * LOG2E
    new_col = lax.broadcasted_iota(jnp.int32, (big, items), 1)
    new_row = lax.broadcasted_iota(jnp.int32, (big, items), 0)
    key_at = lax.broadcasted_iota(jnp.int32, (big, rows_here), 1) + seq * rows_here
    for item in range(req_dev):
        tiled = jnp.concatenate(
            [
                jnp.broadcast_to(queries[2 * item + t : 2 * item + t + 1], (head_count, width))
                for t in range(2)
            ],
            axis=0,
        )
        spread = jnp.where(own_head, tiled, 0.0).astype(BF16)
        old = key_at < lengths[req * req_dev + item]
        recent = (new_col >= 2 * item) & (new_col <= 2 * item + new_row // head_count) & (seq == 0)
        scores = jnp.where(old, nt_dot(spread, cache[item, 0]) * factor, NEG_FILL)
        new_scores = jnp.where(recent, nt_dot(spread, new_keys) * factor, NEG_FILL)
        peak = jnp.maximum(
            jnp.max(scores, axis=1, keepdims=True), jnp.max(new_scores, axis=1, keepdims=True)
        )
        weights = jnp.where(old, jnp.exp2(scores - peak), 0.0)
        new_weights = jnp.where(recent, jnp.exp2(new_scores - peak), 0.0)
        weight_sum = jnp.sum(weights, axis=1, keepdims=True) + jnp.sum(
            new_weights, axis=1, keepdims=True
        )
        value = jnp.dot(
            weights.astype(BF16), cache[item, 1], preferred_element_type=F32
        ) + jnp.dot(new_weights.astype(BF16), new_values, preferred_element_type=F32)
        for kind, field in enumerate((peak, weight_sum, value)):
            kept = jnp.where(own_head, field, 0.0)
            for t in range(2):
                part_all[seq, kind, pl.ds(2 * item + t, 1)] = jnp.sum(
                    kept[t * head_count : (t + 1) * head_count], axis=0, keepdims=True
                )

    part_copies = [
        remote(part_all.at[seq], part_all.at[seq], s_p.at[d - 1], r_p.at[d - 1],
               {"seq": lax.rem(seq + d, seqs)})
        for d in range(1, seqs)
    ]
    for copy in part_copies:
        copy.start()
    for copy in part_copies:
        copy.wait_recv()
    top = reduce(jnp.maximum, [part_all[at, 0] for at in range(seqs)])
    numerator, denominator = 0.0, 0.0
    for at in range(seqs):
        scale = jnp.exp2(part_all[at, 0] - top)
        denominator = denominator + scale * part_all[at, 1]
        numerator = numerator + scale * part_all[at, 2]
    mixed = (numerator / denominator).astype(BF16)
    projected = jnp.dot(mixed, weight[...], preferred_element_type=F32)
    projected = jnp.concatenate([projected, jnp.zeros_like(projected)], axis=0).astype(BF16)
    for at in range(heads):
        proj[at] = projected[:, at * columns : (at + 1) * columns]

    head_copies = []
    for d in range(1, heads):
        target = lax.rem(head + d, heads)
        head_copies.append(
            remote(proj.at[target], proj_in.at[d - 1], s_h.at[d - 1], r_h.at[d - 1], {"head": target})
        )
    for copy in head_copies:
        copy.start()
    total = proj[head].astype(F32)
    for copy in head_copies:
        copy.wait_recv()
    for d in range(1, heads):
        total = total + proj_in[d - 1].astype(F32)
    res_all[req] = total.astype(BF16)

    res_copies = [
        remote(res_all.at[req], res_all.at[req], s_r.at[d - 1], r_r.at[d - 1],
               {"req": lax.rem(req + d, groups)})
        for d in range(1, groups)
    ]
    for copy in res_copies:
        copy.start()
    for copy in res_copies:
        copy.wait_recv()
    final = 0.0
    for group in range(groups):
        final = final + jnp.dot(place[group], res_all[group], preferred_element_type=F32)
    out[...] = final.astype(BF16)
    for copy in fresh_copies + part_copies + head_copies + res_copies:
        copy.wait_send()


def decode_fast(cache_kv, dec_new, out_weight, owner_slot, prompt_lengths, mesh_shape):
    seqs, heads, groups = mesh_shape["seq"], mesh_shape["head"], mesh_shape["req"]
    req_dev, _, rows_here, width = cache_kv.shape
    slot_dev = dec_new.shape[0]
    rows = 2 * slot_dev
    items = 2 * req_dev
    columns = out_weight.shape[1] // heads
    req = lax.axis_index("req")
    fresh = jnp.transpose(dec_new, (1, 0, 2, 3)).reshape(3, rows, width)
    owners = owner_slot.reshape(groups, req_dev)
    item_slot = (owners[:, :, None] * 2 + jnp.arange(2)).reshape(groups, items)
    here = lax.dynamic_index_in_dim(item_slot, req, 0, keepdims=False)
    every = (jnp.arange(groups) * rows)[:, None, None] + jnp.arange(rows)[None, None, :]
    select = (here[None, :, None] == every).astype(BF16)
    filled = jnp.concatenate([item_slot, jnp.full((groups, items), -1, jnp.int32)], axis=1)
    place = (
        filled[:, None, :] == (req * rows + jnp.arange(rows))[None, :, None]
    ).astype(BF16)
    dma = pltpu.SemaphoreType.DMA
    vmem = pltpu.VMEM
    whole = pl.BlockSpec(memory_space=pltpu.VMEM)
    out = pl.pallas_call(
        functools.partial(decode_kernel, groups, seqs, heads),
        out_shape=jax.ShapeDtypeStruct((rows, columns), BF16),
        in_specs=[whole] * 5 + [pl.BlockSpec(memory_space=pltpu.SMEM)],
        out_specs=whole,
        scratch_shapes=[
            vmem((groups, 3, rows, width), BF16),
            vmem((seqs, 3, items, width), F32),
            vmem((heads, 2 * items, columns), BF16),
            vmem((heads - 1, 2 * items, columns), BF16),
            vmem((groups, 2 * items, columns), BF16),
            dma((groups - 1,)), dma((groups - 1,)),
            dma((seqs - 1,)), dma((seqs - 1,)),
            dma((heads - 1,)), dma((heads - 1,)),
            dma((groups - 1,)), dma((groups - 1,)),
        ],
        compiler_params=pltpu.CompilerParams(
            collective_id=1, has_side_effects=True, vmem_limit_bytes=32 * 2**20
        ),
    )(fresh, cache_kv, out_weight, select, place, prompt_lengths)
    return out.reshape(slot_dev, 2, columns)


def on_device(mesh_shape, pre_qkv, cache_kv, dec_new, out_weight, owner_slot, prompt_lengths):
    head_count = pre_qkv.shape[2] // HEAD_DIM
    plain = mesh_shape["seq"] != 4 or head_count % 4
    decode_out = decode_fast(
        cache_kv, dec_new, out_weight, owner_slot, prompt_lengths, mesh_shape
    )
    prefill_out = prefill_block(pre_qkv) if plain else prefill_fast(pre_qkv)
    return (prefill_out, decode_out)


def solution(mesh):
    return jax.shard_map(
        functools.partial(on_device, dict(mesh.shape)),
        mesh=mesh,
        in_specs=(
            P("seq", None, ("head", "req")),
            P("req", None, "seq", "head"),
            P("req", None, None, "head"),
            P("head", "seq"),
            P(),
            P(),
        ),
        out_specs=(P("seq", ("head", "req")), P("req", None, ("seq", "head"))),
        check_vma=False,
    )
```

profile of v0, /device:TPU:0, one launch (start us, length us, event | category | flops | bytes accessed | tf_op | source)
XLA Modules:
  0.0 86.1 jit_solution(14077950834260568106)
XLA Ops:
  0.6 0.0 copy-start.3
  0.6 0.0 copy-start.4
  0.7 0.0 copy-start.1
  0.7 0.0 copy-start.2
  0.7 51.9 %shard_map.77 = bf16[2048,512]{1,0:T(8,128)(2,1)S(1)} custom-call(bf16[3,2048,512]{2,1,0:T(8,128)(2,1)} %bitcast.4), custom_call_target="tpu_custom_call" | custom-call | tf_op jit(solution)/shard_map/pallas_call | solution.py:389
  52.6 0.0 copy-done.3
  52.6 0.1 copy.9
  52.7 0.1 iota_add_fusion
  52.8 0.0 copy-done.4
  52.8 0.1 mul.22
  52.9 0.1 add.54
  53.0 0.1 add.55
  53.1 0.1 add.57
  53.2 0.1 compare_convert_fusion.1.select
  53.3 0.1 compare_convert_fusion.place
  53.3 0.0 copy-done.1
  53.3 0.0 copy-done.2
  53.3 0.0 copy-start
  53.4 1.6 %copy-done = bf16[1024,1024]{1,0:T(8,128)(2,1)S(1)} copy-done((bf16[1024,1024]{1,0:T(8,128)(2,1)S(1)}, bf16[1024,1024]{1,0:T(8,128)(2,1)}, u32[]{:S(2)}) %copy-start) | copy-done | bytes 2097176
  54.9 29.2 %shard_map.78 = bf16[16,256]{1,0:T(8,128)(2,1)S(1)} custom-call(bf16[3,16,1024]{2,1,0:T(8,128)(2,1)S(1)} %reshape.55.fresh, bf16[4,2,64,1024]{3,2,1,0:T(8,128)(2,1)S(1)} %copy-done.1, bf16[1024,1024]{1,0:T(8,128)(2,1)S(1)} %copy-done, bf16[2,8,16]{2,1,0:T(8,128)(2,1)S(1)} %compare_convert_fusion.1.select, bf16[2,16,16]{2,1,0:T(8,128)(2,1)S(1)} %compare_convert_fusion.place, ...), custom_call_target="tpu_custom_call" | custom-call | tf_op jit(solution)/shard_map/pallas_call | solution.py:565
  84.1 0.6 reshape.56
  84.7 1.3 %copy.11 = bf16[2048,512]{1,0:T(8,128)(2,1)} copy(bf16[2048,512]{1,0:T(8,128)(2,1)S(1)} %shard_map.77) | data formatting | bytes 4194304
  (8 shorter events, 0.1 us)
Async XLA Ops:
  0.6 52.0 %copy-start.3 = (bf16[8,3,2,1024]{3,2,1,0:T(2,128)(2,1)S(1)}, bf16[8,3,2,1024]{3,2,1,0:T(2,128)(2,1)}, u32[]{:S(2)}) copy-start(bf16[8,3,2,1024]{3,2,1,0:T(2,128)(2,1)} %param.8) | copy-start | bytes 294916
  0.6 52.2 %copy-start.4 = (s32[8]{0:T(128)S(1)}, s32[8]{0:T(128)}, u32[]{:S(2)}) copy-start(s32[8]{0:T(128)} %param.10) | copy-start | bytes 100
  0.7 52.7 %copy-start.1 = (bf16[4,2,64,1024]{3,2,1,0:T(8,128)(2,1)S(1)}, bf16[4,2,64,1024]{3,2,1,0:T(8,128)(2,1)}, u32[]{:S(2)}) copy-start(bf16[4,2,64,1024]{3,2,1,0:T(8,128)(2,1)} %cache.1) | copy-start | bytes 3145732
  0.7 52.7 %copy-start.2 = (s32[8]{0:T(128)S(1)}, s32[8]{0:T(128)}, u32[]{:S(2)}) copy-start(s32[8]{0:T(128)} %lengths.1) | copy-start | bytes 100
  53.3 1.6 %copy-start = (bf16[1024,1024]{1,0:T(8,128)(2,1)S(1)}, bf16[1024,1024]{1,0:T(8,128)(2,1)}, u32[]{:S(2)}) copy-start(bf16[1024,1024]{1,0:T(8,128)(2,1)} %weight.1) | copy-start | bytes 6291460
where the time goes:
time: 86.2 us; the launch traced here: 86.1 us
  Pallas kernels  81.1 us (94%)
  local copies, waits for them, and re-layouts  3.99 us (5%)
    pallas_call x1, Pallas kernels, prefill_fast(): pl.pallas_call(prefill_kernel, out_shape=jax.ShapeDtypeStruct((row_count,...  51.9 us
    pallas_call x1, Pallas kernels, decode_fast(): pl.pallas_call(functools.partial(decode_kernel, groups, seqs, heads), out...  29.2 us
    unnamed x11, local copies, waits for them, and re-layouts  2.92 us

commit v1 on v0

--- a/solution.py
+++ b/solution.py
@@ -168,21 +168,34 @@
     return lax.dot_general(a, b, (((1,), (1,)), ((), ())), preferred_element_type=F32)
 
 
-def attend(query, parts):
+def attend_all(jobs):
     factor = HEAD_DIM ** (-0.5) * LOG2E
-    scores = []
-    for key, _, allowed in parts:
-        block = nt_dot(query, key)
-        scores.append(block if allowed is None else jnp.where(allowed, block, NEG_FILL))
-    peak = reduce(jnp.maximum, [jnp.max(block, axis=1, keepdims=True) for block in scores])
-    shift = peak * factor
-    total = 0.0
-    for block, (_, value, _) in zip(scores, parts):
-        weights = jnp.exp2(block * factor - shift).astype(BF16)
-        wide = jnp.concatenate([value, jnp.ones_like(value)], axis=1)
-        total = total + jnp.dot(weights, wide, preferred_element_type=F32)
-    weight_sum = total[:, HEAD_DIM:]
-    return total[:, :HEAD_DIM] / weight_sum, shift + jnp.log2(weight_sum)
+
+    def scores_of(job):
+        query, parts, _ = job()
+        scores = []
+        for key, _, allowed in parts:
+            block = nt_dot(query, key)
+            scores.append(block if allowed is None else jnp.where(allowed, block, NEG_FILL))
+        return scores
+
+    def finish(job, scores):
+        _, parts, done = job()
+        peak = reduce(jnp.maximum, [jnp.max(block, axis=1, keepdims=True) for block in scores])
+        shift = peak * factor
+        total = 0.0
+        for block, (_, value, _) in zip(scores, parts):
+            weights = jnp.exp2(block * factor - shift).astype(BF16)
+            wide = jnp.concatenate([value, jnp.ones_like(value)], axis=1)
+            total = total + jnp.dot(weights, wide, preferred_element_type=F32)
+        weight_sum = total[:, HEAD_DIM:]
+        done(total[:, :HEAD_DIM] / weight_sum, shift + jnp.log2(weight_sum))
+
+    scores = scores_of(jobs[0])
+    for at, job in enumerate(jobs):
+        later = scores_of(jobs[at + 1]) if at + 1 < len(jobs) else None
+        finish(job, scores)
+        scores = later
 
 
 def triangle(rows):
@@ -191,9 +204,9 @@
     )
 
 
-def prefill_kernel(
-    qkv, out, near_o, near_l, wide, pick, kv_in, q_in, o_out, l_out, o_in, l_in,
-    s_kv, r_kv, s_q, r_q, s_o, r_o, s_l, r_l,
+def joint_kernel(
+    groups, heads, qkv, fresh, cache, weight, select, place, lengths, out, decode_out, near_o, near_l, wide, pick, kv_in, q_in, o_out, l_out, o_in, l_in,
+    s_kv, r_kv, s_q, r_q, s_o, r_o, s_l, r_l, *decode_scratch,
 ):
     me = lax.axis_index("seq")
     row_count = qkv.shape[1]
@@ -203,11 +216,10 @@
     block = 256
     low, upper = pl.ds(0, half), pl.ds(half, half)
 
-    barrier = pltpu.get_barrier_semaphore()
-    for step in range(1, 4):
-        pl.semaphore_signal(
-            barrier, inc=1, device_id={"seq": lax.rem(me + step, 4)}, device_id_type=MESH
-        )
+    all_here = greet(4, heads, groups)
+    decode = decode_steps(
+        groups, 4, heads, fresh, cache, weight, select, place, lengths, decode_out, *decode_scratch
+    )
 
     order = list(range(half, head_count)) + list(range(half))
     for head in order:
@@ -215,7 +227,7 @@
         for part in range(3):
             wide[...] = qkv[part, :, lanes].astype(F32)
             pick[part, head] = wide[pl.ds(head % 4, sparse, stride=4), :].astype(BF16)
-    pl.semaphore_wait(barrier, 3)
+    all_here()
 
     def kv_copy(heads, target):
         return remote(pick.at[pl.ds(1, 2), heads], kv_in, s_kv, r_kv, {"seq": target})
@@ -251,19 +263,26 @@
             for copy in copies:
                 copy.start()
 
+    next(decode)
     corner = triangle(block)
 
     def near(head):
         lanes = pl.ds(pl.multiple_of(head * HEAD_DIM, HEAD_DIM), HEAD_DIM)
-        for at in range(row_count // block):
+
+        def job(at):
             here = pl.ds(at * block, block)
             parts = [(qkv[1, here, lanes], qkv[2, here, lanes], corner)]
             if at:
                 before = pl.ds(0, at * block)
                 parts.append((qkv[1, before, lanes], qkv[2, before, lanes], None))
-            value, log_sum = attend(qkv[0, here, lanes], parts)
-            near_o[head, here] = value
-            near_l[head, here] = log_sum
+
+            def done(value, log_sum):
+                near_o[head, here] = value
+                near_l[head, here] = log_sum
+
+            return qkv[0, here, lanes], parts, done
+
+        attend_all([functools.partial(job, at) for at in range(row_count // block)])
 
     def near_heads(first, count):
         @pl.loop(first, first + count)
@@ -280,23 +299,33 @@
         near_o.at[head][rows, :] = (one * old_value + two * value) / total
         near_l.at[head][rows, :] = top + jnp.log2(total)
 
-    def own_diagonal(head):
-        for at in range(sparse // block):
+    def own_diagonal():
+        def job(head, at):
             here = pl.ds(at * block, block)
             parts = [(pick[1, head, here], pick[2, head, here], corner)]
             if at:
                 before = pl.ds(0, at * block)
                 parts.append((pick[1, head, before], pick[2, head, before], None))
-            merge(head, at * block, *attend(pick[0, head, here], parts))
+            return pick[0, head, here], parts, functools.partial(merge, head, at * block)
+
+        attend_all(
+            [functools.partial(job, h, at) for h in range(head_count) for at in range(sparse // block)]
+        )
 
     def serve(source, keys):
-        for local in range(half):
-            for at in range(sparse // block):
-                here = pl.ds(at * block, block)
-                value, log_sum = attend(q_in[source - 1, local, here], keys(local))
+        def job(local, at):
+            here = pl.ds(at * block, block)
+
+            def done(value, log_sum):
                 o_out[source - 1, local, here] = value.astype(BF16)
                 l_out[source - 1, local, :, here] = jnp.transpose(log_sum)[:8]
 
+            return q_in[source - 1, local, here], keys(local), done
+
+        attend_all(
+            [functools.partial(job, local, at) for local in range(half) for at in range(sparse // block)]
+        )
+
     def kept(first):
         return lambda local: [(pick[1, first + local], pick[2, first + local], None)]
 
@@ -304,16 +333,20 @@
         return [(kv_in[0, local], kv_in[1, local], None)]
 
     def extra():
-        for local in range(half):
-            for at in range(sparse // block):
-                here = pl.ds(at * block, block)
-                merge(local, at * block, *attend(pick[0, local, here], landed(local)))
+        def job(local, at):
+            here = pl.ds(at * block, block)
+            return pick[0, local, here], landed(local), functools.partial(merge, local, at * block)
+
+        attend_all(
+            [functools.partial(job, local, at) for local in range(half) for at in range(sparse // block)]
+        )
 
     def send_back(source, target):
         for copy in o_copies(source, target):
             copy.start()
 
-    near_heads(0, head_count)
+    near_heads(0, half)
+    next(decode)
 
     @pl.when(me == 0)
     def _():
@@ -321,19 +354,10 @@
         serve(1, kept(half))
         send_back(0, 1)
         kv_copy(upper, 0).wait_recv()
-        for source in (2, 3):
-            q_copy(upper, source, 0).wait_recv()
-            serve(source, lambda local: kept(half)(local) + landed(local))
-            send_back(0, source)
 
     @pl.when(me == 1)
     def _():
         kv_copy(low, 1).wait_recv()
-        for source in (2, 3):
-            q_copy(low, source, 1).wait_recv()
-            serve(source, lambda local: kept(0)(local) + landed(local))
-            send_back(1, source)
-        extra()
 
     @pl.when(me == 2)
     def _():
@@ -344,10 +368,26 @@
     @pl.when(me == 3)
     def _():
         kv_copy(low, 3).wait_recv()
+
+    next(decode)
+    for index, heads_here, first in ((0, upper, half), (1, low, 0)):
+
+        @pl.when(me == index)
+        def _(index=index, heads_here=heads_here, first=first):
+            for source in (2, 3):
+                q_copy(heads_here, source, index).wait_recv()
+                serve(source, lambda local: kept(first)(local) + landed(local))
+                send_back(index, source)
+
+    @pl.when(me % 2 == 1)
+    def _():
         extra()
 
-    for head in range(head_count):
-        own_diagonal(head)
+    next(decode)
+    near_heads(half, half)
+    next(decode)
+
+    own_diagonal()
 
     arriving = {1: [(0, half)], 2: [(1, 0), (0, half)], 3: [(1, 0), (2, half), (0, half)]}
     for index, terms in arriving.items():
@@ -377,40 +417,27 @@
             for target in backs[index]:
                 for copy in o_copies(index, target):
                     copy.wait_send()
-
-
-def prefill_fast(pre_qkv):
-    qkv = jnp.moveaxis(pre_qkv, 1, 0)
-    _, row_count, width = qkv.shape
-    head_count = width // HEAD_DIM
-    half, sparse = head_count // 2, row_count // 4
-    dma = pltpu.SemaphoreType.DMA
-    vmem = pltpu.VMEM
-    return pl.pallas_call(
-        prefill_kernel,
-        out_shape=jax.ShapeDtypeStruct((row_count, width), BF16),
-        in_specs=[pl.BlockSpec(memory_space=pltpu.VMEM)],
-        out_specs=pl.BlockSpec(memory_space=pltpu.VMEM),
-        scratch_shapes=[
-            vmem((head_count, row_count, HEAD_DIM), F32),
-            vmem((head_count, row_count, HEAD_DIM), F32),
-            vmem((row_count, HEAD_DIM), F32),
-            vmem((3, head_count, sparse, HEAD_DIM), BF16),
-            vmem((2, half, sparse, HEAD_DIM), BF16),
-            vmem((3, half, sparse, HEAD_DIM), BF16),
-            vmem((3, half, sparse, HEAD_DIM), BF16),
-            vmem((3, half, 8, sparse), F32),
-            vmem((3, half, sparse, HEAD_DIM), BF16),
-            vmem((3, half, 8, sparse), F32),
-            dma, dma, dma((3,)), dma((3,)), dma((3,)), dma((3,)), dma((3,)), dma((3,)),
-        ],
-        compiler_params=pltpu.CompilerParams(
-            collective_id=0, has_side_effects=True, vmem_limit_bytes=50 * 2**20
-        ),
-    )(qkv)
-
-
-def decode_kernel(
+    next(decode, None)
+
+
+def greet(seqs, heads, groups):
+    seq, head, req = lax.axis_index("seq"), lax.axis_index("head"), lax.axis_index("req")
+    peers = [{"seq": lax.rem(seq + d, seqs)} for d in range(1, seqs)]
+    peers += [{"head": lax.rem(head + d, heads)} for d in range(1, heads)]
+    peers += [{"req": lax.rem(req + d, groups)} for d in range(1, groups)]
+    barrier = pltpu.get_barrier_semaphore()
+    for peer in peers:
+        pl.semaphore_signal(barrier, inc=1, device_id=peer, device_id_type=MESH)
+    return lambda: pl.semaphore_wait(barrier, len(peers))
+
+
+def decode_kernel(groups, seqs, heads, *refs):
+    greet(seqs, heads, groups)()
+    for _ in decode_steps(groups, seqs, heads, *refs):
+        pass
+
+
+def decode_steps(
     groups, seqs, heads,
     fresh, cache, weight, select, place, lengths, out,
     fresh_all, part_all, proj, proj_in, res_all,
@@ -422,14 +449,6 @@
     items = 2 * req_dev
     columns = proj.shape[2]
 
-    barrier = pltpu.get_barrier_semaphore()
-    peers = [{"seq": lax.rem(seq + d, seqs)} for d in range(1, seqs)]
-    peers += [{"head": lax.rem(head + d, heads)} for d in range(1, heads)]
-    peers += [{"req": lax.rem(req + d, groups)} for d in range(1, groups)]
-    for peer in peers:
-        pl.semaphore_signal(barrier, inc=1, device_id=peer, device_id_type=MESH)
-    pl.semaphore_wait(barrier, len(peers))
-
     fresh_copies = [
         remote(fresh, fresh_all.at[req], s_f.at[d - 1], r_f.at[d - 1],
                {"req": lax.rem(req + d, groups)})
@@ -438,6 +457,7 @@
     for copy in fresh_copies:
         copy.start()
     fresh_all[req] = fresh[...]
+    yield
     for copy in fresh_copies:
         copy.wait_recv()
 
@@ -495,6 +515,7 @@
     ]
     for copy in part_copies:
         copy.start()
+    yield
     for copy in part_copies:
         copy.wait_recv()
     top = reduce(jnp.maximum, [part_all[at, 0] for at in range(seqs)])
@@ -517,6 +538,7 @@
         )
     for copy in head_copies:
         copy.start()
+    yield
     total = proj[head].astype(F32)
     for copy in head_copies:
         copy.wait_recv()
@@ -531,17 +553,19 @@
     ]
     for copy in res_copies:
         copy.start()
+    yield
     for copy in res_copies:
         copy.wait_recv()
     final = 0.0
     for group in range(groups):
         final = final + jnp.dot(place[group], res_all[group], preferred_element_type=F32)
     out[...] = final.astype(BF16)
+    yield
     for copy in fresh_copies + part_copies + head_copies + res_copies:
         copy.wait_send()
 
 
-def decode_fast(cache_kv, dec_new, out_weight, owner_slot, prompt_lengths, mesh_shape):
+def run_kernels(pre_qkv, plain, cache_kv, dec_new, out_weight, owner_slot, prompt_lengths, mesh_shape):
     seqs, heads, groups = mesh_shape["seq"], mesh_shape["head"], mesh_shape["req"]
     req_dev, _, rows_here, width = cache_kv.shape
     slot_dev = dec_new.shape[0]
@@ -562,37 +586,66 @@
     dma = pltpu.SemaphoreType.DMA
     vmem = pltpu.VMEM
     whole = pl.BlockSpec(memory_space=pltpu.VMEM)
-    out = pl.pallas_call(
-        functools.partial(decode_kernel, groups, seqs, heads),
-        out_shape=jax.ShapeDtypeStruct((rows, columns), BF16),
-        in_specs=[whole] * 5 + [pl.BlockSpec(memory_space=pltpu.SMEM)],
-        out_specs=whole,
+    smem = pl.BlockSpec(memory_space=pltpu.SMEM)
+    operands = (fresh, cache_kv, out_weight, select, place, prompt_lengths)
+    decode_shape = jax.ShapeDtypeStruct((rows, columns), BF16)
+    decode_scratch = [
+        vmem((groups, 3, rows, width), BF16),
+        vmem((seqs, 3, items, width), F32),
+        vmem((heads, 2 * items, columns), BF16),
+        vmem((heads - 1, 2 * items, columns), BF16),
+        vmem((groups, 2 * items, columns), BF16),
+    ]
+    for peers in (groups, seqs, heads, groups):
+        decode_scratch += [dma((peers - 1,)), dma((peers - 1,))]
+    if plain:
+        out = pl.pallas_call(
+            functools.partial(decode_kernel, groups, seqs, heads),
+            out_shape=decode_shape,
+            in_specs=[whole] * 5 + [smem],
+            out_specs=whole,
+            scratch_shapes=decode_scratch,
+            compiler_params=pltpu.CompilerParams(
+                collective_id=0, has_side_effects=True, vmem_limit_bytes=32 * 2**20
+            ),
+        )(*operands)
+        return prefill_block(pre_qkv), out.reshape(slot_dev, 2, columns)
+    qkv = jnp.moveaxis(pre_qkv, 1, 0)
+    _, row_count, pre_width = qkv.shape
+    head_count = pre_width // HEAD_DIM
+    half, sparse = head_count // 2, row_count // 4
+    prefill_out, out = pl.pallas_call(
+        functools.partial(joint_kernel, groups, heads),
+        out_shape=(jax.ShapeDtypeStruct((row_count, pre_width), BF16), decode_shape),
+        in_specs=[whole] * 6 + [smem],
+        out_specs=(whole, whole),
         scratch_shapes=[
-            vmem((groups, 3, rows, width), BF16),
-            vmem((seqs, 3, items, width), F32),
-            vmem((heads, 2 * items, columns), BF16),
-            vmem((heads - 1, 2 * items, columns), BF16),
-            vmem((groups, 2 * items, columns), BF16),
-            dma((groups - 1,)), dma((groups - 1,)),
-            dma((seqs - 1,)), dma((seqs - 1,)),
-            dma((heads - 1,)), dma((heads - 1,)),
-            dma((groups - 1,)), dma((groups - 1,)),
+            vmem((head_count, row_count, HEAD_DIM), F32),
+            vmem((head_count, row_count, HEAD_DIM), F32),
+            vmem((row_count, HEAD_DIM), F32),
+            vmem((3, head_count, sparse, HEAD_DIM), BF16),
+            vmem((2, half, sparse, HEAD_DIM), BF16),
+            vmem((3, half, sparse, HEAD_DIM), BF16),
+            vmem((3, half, sparse, HEAD_DIM), BF16),
+            vmem((3, half, 8, sparse), F32),
+            vmem((3, half, sparse, HEAD_DIM), BF16),
+            vmem((3, half, 8, sparse), F32),
+            dma, dma, dma((3,)), dma((3,)), dma((3,)), dma((3,)), dma((3,)), dma((3,)),
+            *decode_scratch,
         ],
         compiler_params=pltpu.CompilerParams(
-            collective_id=1, has_side_effects=True, vmem_limit_bytes=32 * 2**20
+            collective_id=0, has_side_effects=True, vmem_limit_bytes=54 * 2**20
         ),
-    )(fresh, cache_kv, out_weight, select, place, prompt_lengths)
-    return out.reshape(slot_dev, 2, columns)
+    )(qkv, *operands)
+    return prefill_out, out.reshape(slot_dev, 2, columns)
 
 
 def on_device(mesh_shape, pre_qkv, cache_kv, dec_new, out_weight, owner_slot, prompt_lengths):
     head_count = pre_qkv.shape[2] // HEAD_DIM
     plain = mesh_shape["seq"] != 4 or head_count % 4
-    decode_out = decode_fast(
-        cache_kv, dec_new, out_weight, owner_slot, prompt_lengths, mesh_shape
-    )
-    prefill_out = prefill_block(pre_qkv) if plain else prefill_fast(pre_qkv)
-    return (prefill_out, decode_out)
+    return run_kernels(
+        pre_qkv, plain, cache_kv, dec_new, out_weight, owner_slot, prompt_lengths, mesh_shape
+    )
 
 
 def solution(mesh):

time: 86.2 us -> 79.4 us (0.921)
  the two profiles are of different devices: /device:TPU:0 before, /device:TPU:26 now
where the time goes in v1:
time: 79.4 us; the launch traced here: 79.2 us
  Pallas kernels  70.1 us (88%)
  local copies, waits for them, and re-layouts  6.33 us (8%)
  other arithmetic  2.08 us (3%)
    pallas_call x1, Pallas kernels, run_kernels(): pl.pallas_call(functools.partial(joint_kernel, groups, heads), out_shape=...  70.1 us
    unnamed x1, local copies, waits for them, and re-layouts  3.04 us

profile of v1, /device:TPU:26, one launch (start us, length us, event | category | flops | bytes accessed | tf_op | source)
XLA Modules:
  0.0 79.2 jit_solution(17498045109343233998)
XLA Ops:
  0.6 0.7 broadcast_multiply_fusion
  1.3 0.1 mul.22
  1.4 0.1 iota_add_fusion
  1.5 0.1 add.57
  1.6 0.1 add.54
  1.6 0.1 add.55
  1.7 0.7 compare_convert_fusion.1.select
  2.4 0.7 compare_convert_fusion.place
  3.1 1.0 %copy.9 = bf16[3,8,2,1024]{3,2,1,0:T(2,128)(2,1)S(1)} copy(bf16[3,8,2,1024]{3,2,0,1:T(2,128)(2,1)} %bitcast.5) | data formatting | bytes 196608 | tf_op jit(solution)/shard_map/transpose | solution.py:576
  4.0 0.7 reshape.55.fresh
  4.7 70.1 %shard_map.77 = (bf16[2048,512]{1,0:T(8,128)(2,1)}, bf16[16,256]{1,0:T(8,128)(2,1)}) custom-call(bf16[3,2048,512]{2,1,0:T(8,128)(2,1)} %bitcast.4, bf16[3,16,1024]{2,1,0:T(8,128)(2,1)} %reshape.55.fresh, bf16[4,2,64,1024]{3,2,1,0:T(8,128)(2,1)} %cache.1, bf16[1024,1024]{1,0:T(8,128)(2,1)} %weight.1, bf16[2,8,16]{2,1,0:T(8,128)(2,1)} %compare_convert_fusion.1.select, ...), custom_call_target="tpu_custom_call" | custom-call | tf_op jit(solution)/shard_map/pallas_call | solution.py:617
  74.8 1.3 %reshape.56 = bf16[8,2,256]{2,1,0:T(2,128)(2,1)} reshape(bf16[16,256]{1,0:T(8,128)(2,1)} %get-tuple-element.5) | data formatting | bytes 16384 | tf_op jit(solution)/shard_map/reshape | solution.py:640
  76.1 3.0 %copy.11 = bf16[2048,512]{1,0:T(8,128)(2,1)} copy(bf16[2048,512]{1,0:T(8,128)(2,1)} %get-tuple-element.8) | data formatting | bytes 4194304
  (6 shorter events, 0.0 us)
